TPU v7x, 32 devices: a whole 2x2x4 slice. The times are simulated.
32 devices in a mesh: dp: 8 (over y, x, core), tensor: 4 (over z).
Axes of the slice: x: 2, y: 2, z: 4, core: 2. Of those that a mesh axis runs over, the one named last changes fastest.
Arguments:
- tokens_in: bfloat16 [8192, 768], P('dp'), may hold values from -6 to 6
- patch_mask: int32 [8192], P('dp'), may hold values 0 or 1
- image_ids: int32 [8192], P('dp'), may hold values from 0 to 10, as said below
- mask_token: float32 [768], replicated, may hold values from -6 to 6
- norm1_gain: float32 [2, 768], replicated, may hold values from 0.5 to 1.5
- norm1_bias: float32 [2, 768], replicated, may hold values from -1.75 to 1.75
- qkv_weight: bfloat16 [2, 768, 3, 768], P(None, None, None, 'tensor'), may hold values from -0.21875 to 0.21875
- qv_bias: float32 [2, 2, 768], P(None, None, 'tensor'), may hold values from -1.75 to 1.75
- out_weight: bfloat16 [2, 768, 768], P(None, 'tensor'), may hold values from -0.625 to 0.625
- out_bias: float32 [2, 768], replicated, may hold values from -1.75 to 1.75
- norm2_gain: float32 [2, 768], replicated, may hold values from 0.5 to 1.5
- norm2_bias: float32 [2, 768], replicated, may hold values from -1.75 to 1.75
- up_weight: bfloat16 [2, 768, 3072], P(None, None, 'tensor'), may hold values from -0.21875 to 0.21875
- up_bias: float32 [2, 3072], P(None, 'tensor'), may hold values from -1.75 to 1.75
- down_weight: bfloat16 [2, 3072, 768], P(None, 'tensor'), may hold values from -0.109375 to 0.109375
- down_bias: float32 [2, 768], replicated, may hold values from -1.75 to 1.75
- out_grad: float32 [8192, 768], P('dp'), may hold values from -6 to 6
Outputs:
- activations: float32 [8192, 768], P('dp')
- tokens_grad: float32 [8192, 768], P('dp')
- mask_token_grad: float32 [768], replicated
- norm1_gain_grad: float32 [2, 768], replicated
- norm1_bias_grad: float32 [2, 768], replicated
- qkv_weight_grad: float32 [2, 768, 3, 768], P(None, None, None, 'tensor')
- qv_bias_grad: float32 [2, 2, 768], P(None, None, 'tensor')
- out_weight_grad: float32 [2, 768, 768], P(None, 'tensor')
- out_bias_grad: float32 [2, 768], replicated
- norm2_gain_grad: float32 [2, 768], replicated
- norm2_bias_grad: float32 [2, 768], replicated
- up_weight_grad: float32 [2, 768, 3072], P(None, None, 'tensor')
- up_bias_grad: float32 [2, 3072], P(None, 'tensor')
- down_weight_grad: float32 [2, 3072, 768], P(None, 'tensor')
- down_bias_grad: float32 [2, 768], replicated
Inputs may be any that keep to these rules, and one draw needn't show every extreme that they name: `image_ids`: on each dp index the rows hold whole images of 100, 196 or 400 patches one after another, numbered 0, 1, 2 and so on; the rows left after the last whole image carry the next number and form one group of their own. On some dp index every image has 100 patches.
All inputs are finite; a program needn't handle non-finite values. No bound on the sum of `patch_mask` on one device may be relied on, other than what follows from the above.
Results may differ from a plain program's by a relative error of at most 0.033.
Values may be sent and summed in bfloat16 or wider, within the bound.
No kernel may reach another device: no remote copies, remote signals or barrier semaphores. Data moves between devices by JAX's collectives and lax.ppermute only.
A program may use at most 128 MiB of HBM per device.

v0:
```python
from functools import partial
import math

import jax
import jax.numpy as jnp
from jax import lax
from jax.sharding import PartitionSpec as P

HD = 64


WIDE = jnp.float32
NARROW = jnp.bfloat16
EPSILON = 1e-06
MASKED = -1e30


def layer_norm(rows_in, gain_row, shift_row):
    centre = rows_in - jnp.mean(rows_in, axis=-1, keepdims=True)
    spread = jnp.mean(centre * centre, axis=-1, keepdims=True)
    return centre * lax.rsqrt(spread + EPSILON) * gain_row + shift_row


def branch_total(partial_sum):
    return lax.psum(partial_sum.astype(jnp.bfloat16), "tensor").astype(jnp.float32)


def back_total(partial_sum):
    return lax.psum(partial_sum.astype(jnp.bfloat16), "tensor").astype(jnp.float32)


def attend_forward(queries, key_rows, value_rows, image_ids):
    row_count, heads_here, head_size = queries.shape
    block_rows = math.gcd(row_count, 512)
    score_scale = head_size ** (-0.5)
    query_blocks = queries.reshape(row_count // block_rows, block_rows, heads_here, head_size)
    id_blocks = image_ids.reshape(row_count // block_rows, block_rows)

    def one_block(inputs):
        query_part, ids_part = inputs
        scores = (
            jnp.einsum("qhd,khd->hqk", query_part, key_rows, preferred_element_type=WIDE)
            * score_scale
        )
        same_image = ids_part[:, None] == image_ids[None, :]
        scores = jnp.where(same_image[None], scores, MASKED)
        row_max = jnp.max(scores, axis=-1, keepdims=True)
        expo_scores = jnp.exp(scores - row_max)
        denom_sum = jnp.sum(expo_scores, axis=-1, keepdims=True)
        weights_low = (expo_scores / denom_sum).astype(NARROW)
        block_out = jnp.einsum("hqk,khd->qhd", weights_low, value_rows, preferred_element_type=WIDE)
        return (block_out, row_max + jnp.log(denom_sum))

    outputs, log_norms = lax.map(one_block, (query_blocks, id_blocks))
    return (outputs.reshape(row_count, heads_here, head_size), log_norms)


def attend_backward(queries, key_rows, value_rows, image_ids, log_norms, grad_out):
    row_count, heads_here, head_size = queries.shape
    block_rows = math.gcd(row_count, 512)
    score_scale = head_size ** (-0.5)
    blocks_total = row_count // block_rows
    query_blocks = queries.reshape(blocks_total, block_rows, heads_here, head_size)
    grad_blocks = grad_out.reshape(blocks_total, block_rows, heads_here, head_size)
    id_blocks = image_ids.reshape(blocks_total, block_rows)

    def one_block(running, inputs):
        grad_key_sum, grad_value_sum = running
        query_part, ids_part, norm_part, grad_part = inputs
        scores = (
            jnp.einsum("qhd,khd->hqk", query_part, key_rows, preferred_element_type=WIDE)
            * score_scale
        )
        same_image = ids_part[:, None] == image_ids[None, :]
        scores = jnp.where(same_image[None], scores, MASKED)
        probs_all = jnp.exp(scores - norm_part)
        probs_low = probs_all.astype(NARROW)
        grad_value_sum = grad_value_sum + jnp.einsum(
            "hqk,qhd->khd", probs_low, grad_part, preferred_element_type=WIDE
        )
        grad_probs = jnp.einsum("qhd,khd->hqk", grad_part, value_rows, preferred_element_type=WIDE)
        grad_scores = probs_all * (
            grad_probs - jnp.sum(probs_all * grad_probs, axis=-1, keepdims=True)
        )
        scores_low = grad_scores.astype(NARROW)
        grad_query = (
            jnp.einsum("hqk,khd->qhd", scores_low, key_rows, preferred_element_type=WIDE)
            * score_scale
        )
        grad_key_sum = (
            grad_key_sum
            + jnp.einsum("hqk,qhd->khd", scores_low, query_part, preferred_element_type=WIDE)
            * score_scale
        )
        return ((grad_key_sum, grad_value_sum), grad_query)

    zero_rows = jnp.zeros((row_count, heads_here, head_size), WIDE)
    (grad_key, grad_value), grad_query = lax.scan(
        one_block, (zero_rows, zero_rows), (query_blocks, id_blocks, log_norms, grad_blocks)
    )
    return (grad_query.reshape(row_count, heads_here, head_size), grad_key, grad_value)


def body(
    tokens_in,
    patch_mask,
    image_ids,
    mask_token,
    norm1_gain,
    norm1_bias,
    qkv_weight,
    qv_bias,
    out_weight,
    out_bias,
    norm2_gain,
    norm2_bias,
    up_weight,
    up_bias,
    down_weight,
    down_bias,
    out_grad,
):
    layer_total = qkv_weight.shape[0]
    local_width = qkv_weight.shape[3]
    head_size = HD
    heads_here = local_width // head_size
    masked_rows = patch_mask == 1
    residual = jnp.where(masked_rows[:, None], mask_token[None, :], tokens_in.astype(WIDE))
    kept_layers = []
    for layer_at in range(layer_total):
        normed = layer_norm(residual, norm1_gain[layer_at], norm1_bias[layer_at]).astype(NARROW)
        projected = jnp.einsum(
            "rd,dcf->rcf", normed, qkv_weight[layer_at], preferred_element_type=WIDE
        )
        row_count = projected.shape[0]
        queries = (
            (projected[:, 0] + qv_bias[layer_at, 0])
            .astype(NARROW)
            .reshape(row_count, heads_here, head_size)
        )
        key_rows = projected[:, 1].astype(NARROW).reshape(row_count, heads_here, head_size)
        value_rows = (
            (projected[:, 2] + qv_bias[layer_at, 1])
            .astype(NARROW)
            .reshape(row_count, heads_here, head_size)
        )
        attended, log_norms = attend_forward(queries, key_rows, value_rows, image_ids)
        attended = attended.reshape(row_count, local_width).astype(NARROW)
        middle = (
            residual
            + branch_total(jnp.dot(attended, out_weight[layer_at], preferred_element_type=WIDE))
            + out_bias[layer_at]
        )
        normed_mid = layer_norm(middle, norm2_gain[layer_at], norm2_bias[layer_at]).astype(NARROW)
        before_act = (
            jnp.dot(normed_mid, up_weight[layer_at], preferred_element_type=WIDE)
            + up_bias[layer_at]
        )
        hidden = jax.nn.gelu(before_act, approximate=False).astype(NARROW)
        kept_layers.append(
            (
                residual,
                normed,
                queries,
                key_rows,
                value_rows,
                attended,
                log_norms,
                middle,
                normed_mid,
                before_act,
                hidden,
            )
        )
        residual = (
            middle
            + branch_total(jnp.dot(hidden, down_weight[layer_at], preferred_element_type=WIDE))
            + down_bias[layer_at]
        )
    activations = residual
    running = out_grad
    layer_grads = [None] * layer_total
    for layer_at in reversed(range(layer_total)):
        (
            residual,
            normed,
            queries,
            key_rows,
            value_rows,
            attended,
            log_norms,
            middle,
            normed_mid,
            before_act,
            hidden,
        ) = kept_layers[layer_at]
        row_count = normed.shape[0]
        bias_down_grad = jnp.sum(running, axis=0)
        grad_low = running.astype(NARROW)
        down_grad = jnp.einsum("rf,rd->fd", hidden, grad_low, preferred_element_type=WIDE)
        grad_hidden = jnp.einsum(
            "rd,fd->rf", grad_low, down_weight[layer_at], preferred_element_type=WIDE
        )
        gelu_pull = jax.vjp(partial(jax.nn.gelu, approximate=False), before_act)[1]
        grad_before = gelu_pull(grad_hidden)[0].astype(NARROW)
        up_grad = jnp.einsum("rd,rf->df", normed_mid, grad_before, preferred_element_type=WIDE)
        bias_up_grad = jnp.sum(grad_before, axis=0, dtype=WIDE)
        grad_normed_mid = back_total(
            jnp.einsum("rf,df->rd", grad_before, up_weight[layer_at], preferred_element_type=WIDE)
        )
        norm_pull = jax.vjp(layer_norm, middle, norm2_gain[layer_at], norm2_bias[layer_at])[1]
        grad_middle, gain2_grad, shift2_grad = norm_pull(grad_normed_mid)
        running = running + grad_middle
        bias_out_grad = jnp.sum(running, axis=0)
        grad_low = running.astype(NARROW)
        out_grad_local = jnp.einsum("rc,rd->cd", attended, grad_low, preferred_element_type=WIDE)
        grad_attended = jnp.einsum(
            "rd,cd->rc", grad_low, out_weight[layer_at], preferred_element_type=WIDE
        ).astype(NARROW)
        grad_attended = grad_attended.reshape(row_count, heads_here, head_size)
        grad_query, grad_key, grad_value = attend_backward(
            queries, key_rows, value_rows, image_ids, log_norms, grad_attended
        )
        grad_projected = (
            jnp.stack((grad_query, grad_key, grad_value), axis=1)
            .reshape(row_count, 3, local_width)
            .astype(NARROW)
        )
        qkv_grad = jnp.einsum("rd,rcf->dcf", normed, grad_projected, preferred_element_type=WIDE)
        bias_qv_grad = jnp.sum(grad_projected[:, 0::2], axis=0, dtype=WIDE)
        grad_normed = back_total(
            jnp.einsum(
                "rcf,dcf->rd", grad_projected, qkv_weight[layer_at], preferred_element_type=WIDE
            )
        )
        norm_pull = jax.vjp(layer_norm, residual, norm1_gain[layer_at], norm1_bias[layer_at])[1]
        grad_residual, gain1_grad, shift1_grad = norm_pull(grad_normed)
        running = running + grad_residual
        layer_grads[layer_at] = (
            gain1_grad,
            shift1_grad,
            qkv_grad,
            bias_qv_grad,
            out_grad_local,
            bias_out_grad,
            gain2_grad,
            shift2_grad,
            up_grad,
            bias_up_grad,
            down_grad,
            bias_down_grad,
        )
    stacked = [jnp.stack(group) for group in zip(*layer_grads)]
    fill_grad = jnp.sum(jnp.where(masked_rows[:, None], running, 0.0), axis=0)
    input_grad_rows = jnp.where(masked_rows[:, None], 0.0, running)
    summed = (
        lax.psum(fill_grad.astype(jnp.bfloat16), "dp").astype(jnp.float32),
        lax.psum(stacked[0].astype(jnp.bfloat16), "dp").astype(jnp.float32),
        lax.psum(stacked[1].astype(jnp.bfloat16), "dp").astype(jnp.float32),
        lax.psum(stacked[2].astype(jnp.bfloat16), "dp").astype(jnp.float32),
        lax.psum(stacked[3].astype(jnp.bfloat16), "dp").astype(jnp.float32),
        lax.psum(stacked[4].astype(jnp.bfloat16), "dp").astype(jnp.float32),
        lax.psum(stacked[5].astype(jnp.bfloat16), "dp").astype(jnp.float32),
        lax.psum(stacked[6].astype(jnp.bfloat16), "dp").astype(jnp.float32),
        lax.psum(stacked[7].astype(jnp.bfloat16), "dp").astype(jnp.float32),
        lax.psum(stacked[8].astype(jnp.bfloat16), "dp").astype(jnp.float32),
        lax.psum(stacked[9].astype(jnp.bfloat16), "dp").astype(jnp.float32),
        lax.psum(stacked[10].astype(jnp.bfloat16), "dp").astype(jnp.float32),
        lax.psum(stacked[11].astype(jnp.bfloat16), "dp").astype(jnp.float32),
    )
    return (
        activations,
        input_grad_rows,
        summed[0],
        summed[1],
        summed[2],
        summed[3],
        summed[4],
        summed[5],
        summed[6],
        summed[7],
        summed[8],
        summed[9],
        summed[10],
        summed[11],
        summed[12],
    )


def solution(mesh):
    placed = (
        P("dp", None),
        P("dp"),
        P("dp"),
        P(),
        P(),
        P(),
        P(None, None, None, "tensor"),
        P(None, None, "tensor"),
        P(None, "tensor", None),
        P(),
        P(),
        P(),
        P(None, None, "tensor"),
        P(None, "tensor"),
        P(None, "tensor", None),
        P(),
        P("dp", None),
    )
    return jax.shard_map(
        body,
        mesh=mesh,
        in_specs=placed,
        out_specs=(
            P("dp", None),
            P("dp", None),
            P(),
            P(),
            P(),
            P(None, None, None, "tensor"),
            P(None, None, "tensor"),
            P(None, "tensor", None),
            P(),
            P(),
            P(),
            P(None, None, "tensor"),
            P(None, "tensor"),
            P(None, "tensor", None),
            P(),
        ),
        check_vma=False,
    )
```

profile of v0, /device:TPU:1, one launch (start us, length us, event | category | flops | bytes accessed | tf_op | source)
XLA Modules:
  0.0 885.3 jit_solution(15421244483654925517)
XLA Ops:
  23.0 13.1 %while.54 = (s32[]{:T(128)}, bf16[2,512,3,64]{1,3,2,0:T(8,128)(2,1)}, f32[2,3,512,1]{2,1,3,0:T(4,128)S(1)}, s32[2,512]{1,0:T(2,128)S(1)}, s32[1024]{0:T(1024)S(1...) while((s32[]{:T(128)}, ...), condition=%wide.region_5.6_spmd, body=%wide.region_2.5_spmd.sunk | while | flops 422050304 | bytes 25563308 | solution.py:54
  42.9 68.0 %all-reduce.12.cloned.1.call-done = bf16[1024,768]{1,0:T(8,128)(2,1)} async-done(((bf16[1024,768]{1,0:T(8,128)(2,1)}), bf16[1024,768]{1,0:T(8,128)(2,1)}) %all-reduce.12.cloned.1.call-update) | async-done | bytes 1572880 | tf_op jit(solution)/shard_map/psum | solution.py:25
  117.2 9.1 %multiply_convert_fusion.3 = (bf16[1024,768]{1,0:T(8,128)(2,1)S(1)}, f32[1024,768]{1,0:T(8,128)}, f32[1024,768]{1,0:T(8,128)}) fusion(f32[768]{0:T(1024)S(1)} %copy-done.149, bf16[1024,768]{1,0:T(8,128)(2,1)S(1)} %add_convert_fusion.4, bf16[2,768,768]{2,1,0:T(8,128)(2,1)S(1)} %copy-done.156), kind=kOutput, calls=%fused_computation.161 | convolution fusion | flops 1259864064 | bytes 10620928 | tf_op jit(solution)/shard_map/dot_general | solution.py:156
  132.5 65.8 %all-reduce.14.cloned.1.call-done = bf16[1024,768]{1,0:T(8,128)(2,1)} async-done(((bf16[1024,768]{1,0:T(8,128)(2,1)}), bf16[1024,768]{1,0:T(8,128)(2,1)}) %all-reduce.14.cloned.1.call-update) | async-done | bytes 1572880 | tf_op jit(solution)/shard_map/psum | solution.py:25
  205.8 11.6 %while.55 = (s32[]{:T(128)}, bf16[2,512,3,64]{1,3,2,0:T(8,128)(2,1)S(1)}, f32[2,3,512,1]{2,1,3,0:T(4,128)S(1)}, s32[2,512]{1,0:T(2,128)S(1)}, s32[1024]{0:T(1024...) while((s32[]{:T(128)}, ...), condition=%wide.region_15.16_spmd, body=%wide.region_12.15_spmd.sunk | while | flops 422050304 | bytes 22417524 | solution.py:54
  221.2 68.1 %all-reduce.16.cloned.1.call-done = bf16[1024,768]{1,0:T(8,128)(2,1)} async-done(((bf16[1024,768]{1,0:T(8,128)(2,1)}), bf16[1024,768]{1,0:T(8,128)(2,1)}) %all-reduce.16.cloned.1.call-update) | async-done | bytes 1572880 | tf_op jit(solution)/shard_map/psum | solution.py:25
  295.0 20.2 %multiply_convert_fusion.2 = (bf16[1024,768]{1,0:T(8,128)(2,1)}, f32[1024,768]{1,0:T(8,128)S(1)}, f32[1024,768]{1,0:T(8,128)S(1)}) fusion(f32[768]{0:T(1024)S(1)} %copy-done.151, bf16[1024,768]{1,0:T(8,128)(2,1)S(1)} %add_convert_fusion.2, bf16[2,768,768]{2,1,0:T(8,128)(2,1)S(1)} %copy-done.157), kind=kOutput, calls=%fused_computation.142 | convolution fusion | flops 1259864064 | bytes 10620928 | tf_op jit(solution)/shard_map/dot_general | solution.py:156
  322.2 68.0 %all-reduce.18.cloned.1.call-done = bf16[1024,768]{1,0:T(8,128)(2,1)} async-done(((bf16[1024,768]{1,0:T(8,128)(2,1)}), bf16[1024,768]{1,0:T(8,128)(2,1)}) %all-reduce.18.cloned.1.call-update) | async-done | bytes 1572880 | tf_op jit(solution)/shard_map/psum | solution.py:29
  399.9 22.5 %while.56 = (s32[]{:T(128)}, f32[1024,3,64]{0,2,1:T(8,128)S(1)}, f32[1024,3,64]{0,2,1:T(8,128)}, bf16[2,512,3,64]{1,3,2,0:T(8,128)(2,1)S(1)}, bf16[2,512,3,64]{1...) while((s32[]{:T(128)}, f32[1024,3,64]{0,2,1:T(8,128)S(1)}, ...), condition=%wide.region_25.26_spmd.clone, body=%wide.region_23.25_spmd.clone.sunk | while | flops 1031830016 | bytes 54845608 | solution.py:98
  411.8 4.0 fusion.285
  425.2 3.9 bitcast_convert_fusion.1
  430.5 67.0 %all-reduce.20.cloned.1.call-done = bf16[1024,768]{1,0:T(8,128)(2,1)} async-done(((bf16[1024,768]{1,0:T(8,128)(2,1)}), bf16[1024,768]{1,0:T(8,128)(2,1)}) %all-reduce.20.cloned.1.call-update) | async-done | bytes 1572880 | tf_op jit(solution)/shard_map/psum | solution.py:29
  513.7 4.1 convolution_convert_fusion.2
  526.7 55.2 %all-reduce.22.cloned.1.call-done = bf16[1024,768]{1,0:T(8,128)(2,1)} async-done(((bf16[1024,768]{1,0:T(8,128)(2,1)}), bf16[1024,768]{1,0:T(8,128)(2,1)}) %all-reduce.22.cloned.1.call-update) | async-done | bytes 1572880 | tf_op jit(solution)/shard_map/psum | solution.py:29
  598.6 21.5 %while.57 = (s32[]{:T(128)}, f32[1024,3,64]{0,2,1:T(8,128)S(1)}, f32[1024,3,64]{0,2,1:T(8,128)}, bf16[2,512,3,64]{1,3,2,0:T(8,128)(2,1)}, bf16[2,512,3,64]{1,3,2...) while((s32[]{:T(128)}, f32[1024,3,64]{0,2,1:T(8,128)S(1)}, ...), condition=%wide.region_34.35_spmd.clone, body=%wide.region_32.34_spmd.clone.sunk | while | flops 1031830016 | bytes 65855796 | solution.py:98
  624.0 3.8 bitcast_convert_fusion
  634.6 3.2 fusion.135
  639.2 3.4 fusion.114
  659.1 90.4 %all-reduce.26.cloned.1.call-done = (bf16[1024,768]{1,0:T(8,128)(2,1)}, bf16[1024,768]{1,0:T(8,128)(2,1)}) async-done(((bf16[1024,768]{1,0:T(8,128)(2,1)}, bf16[1024,768]{1,0:T(8,128)(2,1)}), (bf16[1024,768]{1,0:T(8,128)(2,1)}, bf16[1024,768]{1,0:T(8,128)(2,1)})) %all-reduce.26.cloned.1.call-update) | async-done | bytes 3145744 | tf_op jit(solution)/shard_map/psum | solution.py:25
  756.4 3.1 select_reduce_fusion
  759.5 22.8 %all-reduce = (bf16[768]{0:T(1024)(128)(2,1)S(1)}, bf16[2,768]{1,0:T(2,128)(2,1)S(1)}, bf16[2,768]{1,0:T(2,128)(2,1)S(1)}, bf16[2,2,192]{2,1,0:T(2,128)(2,1)S(1)...) all-reduce(bf16[768]{0:T(1024)(128)(2,1)S(1)} %get-tuple-element.46, ...), channel_id=1, replica_groups=mesh['dp'=8,'tensor'=4] {'dp'}, use_global_device_ids=true, to_apply=%region_39.40 | all-reduce | flops 12288 | bytes 49152 | tf_op jit(solution)/shard_map/psum | solution.py:257
  787.7 4.1 broadcast_select_fusion
  793.7 73.5 %all-reduce.24.cloned.1.call-done = (bf16[2,768,3,192]{1,3,2,0:T(8,128)(2,1)}, bf16[2,192,768]{2,1,0:T(8,128)(2,1)}, bf16[2,768,768]{2,1,0:T(8,128)(2,1)}, bf16[2,768,768]{2,1,0:T(8,128)(2,1)}) async-done(((bf16[2,768,3,192]{1,3,2,0:T(8,128)(2,1)}, bf16[2,192,768]{2,1,0:T(8,128)(2,1)}, bf16[2,768,768]{2,1,0:T(8,128)(2,1)}, bf16[2,768,768]{2,1,0:T(8,128)(2,1)}), (bf16[2,768,3,192]{1,3,2,0:T(8,128)(2,1)}, ...) | async-done | bytes 7077904 | tf_op jit(solution)/shard_map/psum | solution.py:260
  869.5 3.6 convert_element_type.264
  (585 shorter events, 226.6 us)
Async XLA Ops:
  7.2 103.7 %all-reduce.12.cloned.1.call-start = ((), (), s32[]{:S(2)}) async-start(), calls=%async_computation | async-start | bytes 3145728 | tf_op jit(solution)/shard_map/psum | solution.py:25
  36.1 77.2 %copy-start.6 = (bf16[1024,3,64]{0,2,1:T(8,128)(2,1)}, bf16[1024,3,64]{0,2,1:T(8,128)(2,1)S(1)}, u32[]{:S(2)}) copy-start(bf16[1024,3,64]{0,2,1:T(8,128)(2,1)S(1)} %get-tuple-element.901) | copy-start | bytes 1179652
  40.6 157.7 %all-reduce.14.cloned.1.call-start = ((), (), s32[]{:S(2)}) async-start(), calls=%async_computation.1 | async-start | bytes 3145728 | tf_op jit(solution)/shard_map/psum | solution.py:25
  41.6 156.7 %copy-start.85 = (f32[768]{0:T(1024)}, f32[768]{0:T(1024)S(1)}, u32[]{:S(2)}) copy-start(f32[768]{0:T(1024)S(1)} %get-tuple-element.362) | copy-start | bytes 9220
  127.4 70.9 %copy-start.89 = (pred[1024]{0:T(1024)(128)(4,1)S(1)}, pred[1024]{0:T(1024)(128)(4,1)}, u32[]{:S(2)}) copy-start(pred[1024]{0:T(1024)(128)(4,1)} %copy-done.87) | copy-start | bytes 3076
  130.0 159.3 %all-reduce.16.cloned.1.call-start = ((), (), s32[]{:S(2)}) async-start(), calls=%async_computation.2 | async-start | bytes 3145728 | tf_op jit(solution)/shard_map/psum | solution.py:25
  218.0 71.3 %copy-start.19 = (bf16[2,512,3,64]{1,3,2,0:T(8,128)(2,1)}, bf16[2,512,3,64]{1,3,2,0:T(8,128)(2,1)S(1)}, u32[]{:S(2)}) copy-start(bf16[2,512,3,64]{1,3,2,0:T(8,128)(2,1)S(1)} %get-tuple-element.905) | copy-start | bytes 1179652
  218.0 71.3 %copy-start.30 = (bf16[1024,3,64]{0,2,1:T(8,128)(2,1)}, bf16[1024,3,64]{0,2,1:T(8,128)(2,1)S(1)}, u32[]{:S(2)}) copy-start(bf16[1024,3,64]{0,2,1:T(8,128)(2,1)S(1)} %get-tuple-element.912) | copy-start | bytes 1179652
  218.0 71.3 %copy-start.126 = (f32[768]{0:T(1024)S(1)}, f32[768]{0:T(1024)}, u32[]{:S(2)}) copy-start(f32[768]{0:T(1024)} %get-tuple-element.361) | copy-start | bytes 9220
  221.0 169.2 %all-reduce.18.cloned.1.call-start = ((), (), s32[]{:S(2)}) async-start(), calls=%async_computation.3 | async-start | bytes 3145728 | tf_op jit(solution)/shard_map/psum | solution.py:29
  292.2 102.8 %copy-start.2 = (f32[1024,768]{1,0:T(8,128)}, f32[1024,768]{1,0:T(8,128)S(1)}, u32[]{:S(2)}) copy-start(f32[1024,768]{1,0:T(8,128)S(1)} %get-tuple-element.473) | copy-start | bytes 9437188
  321.9 175.6 %all-reduce.20.cloned.1.call-start = ((), (), s32[]{:S(2)}) async-start(), calls=%async_computation.4 | async-start | bytes 3145728 | tf_op jit(solution)/shard_map/psum | solution.py:29
  425.2 72.2 %copy-start.5 = (f32[1024,768]{1,0:T(8,128)S(1)}, f32[1024,768]{1,0:T(8,128)}, u32[]{:S(2)}) copy-start(f32[1024,768]{1,0:T(8,128)} %copy-done.4) | copy-start | bytes 9437188
  425.2 72.2 %copy-start.99 = (f32[1024]{0:T(1024)S(1)}, f32[1024]{0:T(1024)}, u32[]{:S(2)}) copy-start(f32[1024]{0:T(1024)} %copy-done.98) | copy-start | bytes 12292
  425.2 72.2 %copy-start.105 = (f32[768]{0:T(1024)S(1)}, f32[768]{0:T(1024)}, u32[]{:S(2)}) copy-start(f32[768]{0:T(1024)} %get-tuple-element.500) | copy-start | bytes 9220
  429.1 152.8 %all-reduce.22.cloned.1.call-start = ((), (), s32[]{:S(2)}) async-start(), calls=%async_computation.5 | async-start | bytes 3145728 | tf_op jit(solution)/shard_map/psum | solution.py:29
  513.6 235.9 %all-reduce.26.cloned.1.call-start = ((), (), s32[]{:S(2)}) async-start(), calls=%async_computation.7 | async-start | bytes 6291456 | tf_op jit(solution)/shard_map/psum | solution.py:25
  526.7 58.4 %copy-start.118 = (f32[1024]{0:T(1024)S(1)}, f32[1024]{0:T(1024)}, u32[]{:S(2)}) copy-start(f32[1024]{0:T(1024)} %copy-done.117) | copy-start | bytes 12292
  526.7 58.4 %copy-start.110 = (f32[1024]{0:T(1024)S(1)}, f32[1024]{0:T(1024)}, u32[]{:S(2)}) copy-start(f32[1024]{0:T(1024)} %copy-done.109) | copy-start | bytes 12292
  627.8 239.4 %all-reduce.24.cloned.1.call-start = ((), (), s32[]{:S(2)}) async-start(), calls=%async_computation.6 | async-start | bytes 14155776 | tf_op jit(solution)/shard_map/psum | solution.py:260
  656.6 94.8 %copy-start.95 = (f32[1024]{0:T(1024)S(1)}, f32[1024]{0:T(1024)}, u32[]{:S(2)}) copy-start(f32[1024]{0:T(1024)} %copy-done.94) | copy-start | bytes 12292
  656.6 94.8 %copy-start.101 = (f32[768]{0:T(1024)S(1)}, f32[768]{0:T(1024)}, u32[]{:S(2)}) copy-start(f32[768]{0:T(1024)} %copy-done.100) | copy-start | bytes 9220
  657.6 96.6 %copy-start.116 = (f32[1024]{0:T(1024)S(1)}, f32[1024]{0:T(1024)}, u32[]{:S(2)}) copy-start(f32[1024]{0:T(1024)} %copy-done.115) | copy-start | bytes 12292
  657.6 96.7 %copy-start.108 = (f32[1024]{0:T(1024)S(1)}, f32[1024]{0:T(1024)}, u32[]{:S(2)}) copy-start(f32[1024]{0:T(1024)} %copy-done.107) | copy-start | bytes 12292
  (162 other events, 987.6 us)
Sparse Core Ops, SparseCore 0:
  40.8 70.0 all-reduce.11
  130.1 68.1 all-reduce.13
  221.1 68.1 all-reduce.15
  322.0 68.1 all-reduce.17
  429.3 68.1 all-reduce.19
  513.8 68.1 all-reduce.21
  627.9 121.5 all-reduce.25
  754.4 112.8 all-reduce.23
where the time goes:
time: 894 us; the launch traced here: 885 us
  waiting for transfers between devices  556 us (62%)
  matrix products  126 us (14%)
  other arithmetic  109 us (12%)
  local copies, waits for them, and re-layouts  52.5 us (6%)
  blocking collectives  22.8 us (3%)
  between operations  16.2 us (2%)
    psum x4, waiting for transfers between devices, branch_total(): lax.psum(partial_sum.astype(jnp.bfloat16), 'tensor').astype(jnp.float32)  292 us
    psum x3, waiting for transfers between devices, back_total(): lax.psum(partial_sum.astype(jnp.bfloat16), 'tensor').astype(jnp.float32)  190 us
    psum x1, waiting for transfers between devices, body(): lax.psum(stacked[2].astype(jnp.bfloat16), 'dp').astype(jnp.float32)  73.5 us
    dot_general x2, matrix products, body(): jnp.dot(normed_mid, up_weight[layer_at], preferred_element_type=WIDE)  29.3 us
    unnamed x332, local copies, waits for them, and re-layouts  26.1 us
    reduce_sum x12, other arithmetic, layer_norm(): return centre * lax.rsqrt(spread + EPSILON) * gain_row + shift_row  23.8 us
    psum x1, blocking collectives, body(): lax.psum(fill_grad.astype(jnp.bfloat16), 'dp').astype(jnp.float32)  22.8 us
  transfers between devices with their start and end apart: 8, of which 8 were waited for; matrix products, arithmetic and copies ran while one was open for 7% of the time, Pallas kernels for 0%

commit v1 on v0

v1 whole, which is shorter than its diff:
```python
from functools import partial

import jax
import jax.numpy as jnp
from jax import lax
from jax.experimental import pallas as pl
from jax.experimental.pallas import tpu as pltpu
from jax.sharding import PartitionSpec as P

AXES = ("dp", "tensor")
HD = 64
WIDE = jnp.float32
NARROW = jnp.bfloat16
EPSILON = 1e-06
MASKED = -1e30
NN = ((1,), (0,))
NT = ((1,), (1,))
TN = ((0,), (0,))


def dot(a, b, dims=NN):
    return lax.dot_general(a, b, (dims, ((), ())), preferred_element_type=WIDE)


def call(kernel, outs, *args, scratch=(), flops=0, exps=0):
    size = lambda x: x.size * x.dtype.itemsize
    moved = sum(size(x) for x in args) + sum(size(x) for x in outs)
    return pl.pallas_call(
        kernel,
        out_shape=outs,
        in_specs=[pl.BlockSpec(memory_space=pltpu.VMEM)] * len(args),
        out_specs=[pl.BlockSpec(memory_space=pltpu.VMEM)] * len(outs),
        scratch_shapes=list(scratch),
        compiler_params=pltpu.CompilerParams(vmem_limit_bytes=48 * 2**20),
        cost_estimate=pl.CostEstimate(flops=flops, bytes_accessed=moved, transcendentals=exps),
    )(*args)


def shape(s, kind=NARROW):
    return jax.ShapeDtypeStruct(s, kind)


def attend_rows(qkv_ref, at, ids_col, ids_row, q_rows, width):
    same = ids_col == ids_row
    bias = jnp.where(same, 0.0, MASKED)
    outs, lses = [], []
    for head in range(width // HD):
        cols = slice(head * HD, head * HD + HD)
        q = qkv_ref[pl.ds(at, q_rows), cols]
        k = qkv_ref[:, width + head * HD : width + head * HD + HD]
        v = qkv_ref[:, 2 * width + head * HD : 2 * width + head * HD + HD]
        s = dot(k, q * jnp.asarray(HD**-0.5, NARROW), NT) + bias
        top = jnp.max(s, axis=0, keepdims=True)
        e = jnp.exp(s - top)
        total = jnp.sum(e, axis=0, keepdims=True)
        o = dot(e.astype(NARROW), v, TN)
        o = o * jnp.transpose(1.0 / total)
        outs.append(o)
        lses.append(top + jnp.log(total))
    return jnp.concatenate(outs, axis=1), jnp.concatenate(lses, axis=0)


def qkv_kernel(mine_ref, other_ref, w_ref, b_ref, out_ref):
    half = mine_ref.shape[0]
    for ref, at in ((mine_ref, 0), (other_ref, half)):
        for r in range(0, half, 256):
            y = dot(ref[r : r + 256, :], w_ref[...]) + b_ref[...]
            out_ref[at + r : at + r + 256, :] = y.astype(NARROW)


def make_attn_fwd(q0, q1, width, block):
    def kernel(qkv_ref, idc_ref, idr_ref, w_ref, att_ref, lse_ref, part_ref):
        def step(i, _):
            at = pl.multiple_of(q0 + i * block, block)
            o, lse = attend_rows(
                qkv_ref, at, idc_ref[...], idr_ref[:, pl.ds(at, block)], block, width
            )
            low = o.astype(NARROW)
            r = pl.multiple_of(i * block, block)
            att_ref[pl.ds(r, block), :] = low
            lse_ref[:, pl.ds(r, block)] = lse
            part_ref[pl.ds(r, block), :] = dot(low, w_ref[...], NT).astype(NARROW)
            return 0

        lax.fori_loop(0, (q1 - q0) // block, step, 0)

    return kernel


def stats(x):
    mean = jnp.mean(x, axis=-1, keepdims=True)
    centre = x - mean
    spread = jnp.mean(centre * centre, axis=-1, keepdims=True)
    return centre, lax.rsqrt(spread + EPSILON)


def norm_kernel(x_ref, a_ref, b_ref, bias_ref, gain_ref, shift_ref, h_ref, n_ref):
    for r in range(0, x_ref.shape[0], 128):
        rows = slice(r, r + 128)
        h = x_ref[rows, :] + (a_ref[rows, :].astype(WIDE) + b_ref[rows, :].astype(WIDE)) + bias_ref[...]
        h_ref[rows, :] = h
        centre, inv = stats(h)
        n_ref[rows, :] = (centre * inv * gain_ref[...] + shift_ref[...]).astype(NARROW)


def fold(x):
    return jnp.sum(x.reshape(x.shape[0] // 8, 8, x.shape[1]), axis=0)


def make_norm_back(last):
    def kernel(g_ref, a_ref, b_ref, x_ref, gain_ref, *refs):
        if last:
            mask_ref, low_ref, sums_ref = refs
        else:
            out_ref, low_ref, sums_ref = refs
        half, d = x_ref.shape
        gain_sum = jnp.zeros((8, d), WIDE)
        shift_sum = jnp.zeros((8, d), WIDE)
        out_sum = jnp.zeros((8, d), WIDE)
        for r in range(0, half, 64):
            rows = slice(r, r + 64)
            gn = a_ref[rows, :].astype(WIDE) + b_ref[rows, :].astype(WIDE)
            centre, inv = stats(x_ref[rows, :])
            xhat = centre * inv
            e = gn * gain_ref[...]
            mean_e = jnp.mean(e, axis=-1, keepdims=True)
            mean_ex = jnp.mean(e * xhat, axis=-1, keepdims=True)
            out = g_ref[rows, :] + inv * (e - mean_e - xhat * mean_ex)
            if last:
                masked = mask_ref[rows, :] == 1
                low_ref[rows, :] = jnp.where(masked, 0.0, out).astype(NARROW)
                out = jnp.where(masked, out, 0.0)
            else:
                out_ref[rows, :] = out
                low_ref[rows, :] = out.astype(NARROW)
            gain_sum += fold(gn * xhat)
            shift_sum += fold(gn)
            out_sum += fold(out)
        total = lambda x: jnp.sum(x, axis=0, keepdims=True)
        sums = [total(gain_sum), total(shift_sum), total(out_sum)]
        if last:
            sums_ref[...] = jnp.concatenate(sums + [jnp.zeros((5, d), WIDE)], axis=0)
        else:
            sums_ref[...] = jnp.concatenate(sums + [jnp.zeros((5, d), WIDE)], axis=0)
            low_ref[half:, :] = jnp.concatenate(sums + [jnp.zeros((13, d), WIDE)], axis=0).astype(NARROW)

    return kernel


def cast_kernel(g_ref, low_ref):
    half, d = g_ref.shape
    total = jnp.zeros((8, d), WIDE)
    for r in range(0, half, 64):
        g = g_ref[r : r + 64, :]
        low_ref[r : r + 64, :] = g.astype(NARROW)
        total += fold(g)
    zero = jnp.zeros((1, d), WIDE)
    sums = [zero, zero, jnp.sum(total, axis=0, keepdims=True), jnp.zeros((13, d), WIDE)]
    low_ref[half:, :] = jnp.concatenate(sums, axis=0).astype(NARROW)


def first_kernel(x_ref, mask_ref, fill_ref, gain_ref, shift_ref, h_ref, n_ref):
    for r in range(0, x_ref.shape[0], 128):
        rows = slice(r, r + 128)
        h = jnp.where(mask_ref[rows, :] == 1, fill_ref[...], x_ref[rows, :].astype(WIDE))
        h_ref[rows, :] = h
        centre, inv = stats(h)
        n_ref[rows, :] = (centre * inv * gain_ref[...] + shift_ref[...]).astype(NARROW)


ERF = (0.254829592, -0.284496736, 1.421413741, -1.453152027, 1.061405429)


def gelu_and_slope(x):
    bell = jnp.exp(x * x * -0.5)
    t = 1.0 / (1.0 + (0.3275911 * 0.7071067811865476) * jnp.abs(x))
    tail = t * (ERF[0] + t * (ERF[1] + t * (ERF[2] + t * (ERF[3] + t * ERF[4]))))
    tail = 0.5 * (tail * bell)
    phi = jnp.where(x < 0.0, tail, 1.0 - tail)
    return x * phi, phi + x * (0.3989422804014327 * bell)


def mlp_kernel(n_ref, up_ref, bias_ref, down_ref, hid_ref, slope_ref, part_ref):
    for r in range(0, n_ref.shape[0], 256):
        rows = slice(r, r + 256)
        for f in range(0, up_ref.shape[1], 256):
            cols = slice(f, f + 256)
            x = dot(n_ref[rows, :], up_ref[:, cols]) + bias_ref[:, cols]
            y, slope = gelu_and_slope(x)
            hid_ref[rows, cols] = y.astype(NARROW)
            slope_ref[rows, cols] = slope.astype(NARROW)
        part_ref[rows, :] = dot(hid_ref[rows, :], down_ref[...]).astype(NARROW)


def mlp_back_kernel(g_ref, down_ref, slope_ref, up_ref, gb_ref, part_ref, sum_ref):
    total = jnp.zeros((8, down_ref.shape[0]), WIDE)
    for r in range(0, gb_ref.shape[0], 256):
        rows = slice(r, r + 256)
        dh = dot(g_ref[rows, :], down_ref[...], NT)
        gb = (dh * slope_ref[rows, :].astype(WIDE)).astype(NARROW)
        gb_ref[rows, :] = gb
        total += fold(gb.astype(WIDE))
        part_ref[rows, :] = dot(gb, up_ref[...], NT).astype(NARROW)
    sum_ref[...] = jnp.broadcast_to(jnp.sum(total, axis=0, keepdims=True), sum_ref.shape)


def pair_grad_kernel(am_ref, ao_ref, bm_ref, bo_ref, out_ref):
    for f in range(0, out_ref.shape[0], 192):
        cols = slice(f, f + 192)
        half = am_ref.shape[0]
        y = dot(am_ref[:, cols], bm_ref[0:half, :], TN) + dot(ao_ref[:, cols], bo_ref[0:half, :], TN)
        out_ref[cols, :] = y.astype(NARROW)


def make_attn_back(width, block):
    heads = width // HD

    def kernel(gm_ref, go_ref, w_ref, qkv_ref, att_m_ref, att_o_ref, lse_m_ref, lse_o_ref, idc_ref, idr_ref,
               wq_ref, d_ref, sum_ref, part_m_ref, part_o_ref, ga_ref, dqt_ref, dd_ref):
        rows = qkv_ref.shape[0]
        half = rows // 2
        for ref, att, at in ((gm_ref, att_m_ref, 0), (go_ref, att_o_ref, half)):
            ga = dot(ref[0:half, :], w_ref[...]).astype(NARROW)
            ga_ref[at : at + half, :] = ga
            x = ga.astype(WIDE) * att[...].astype(WIDE)
            per = [jnp.sum(x[:, HD * i : HD * i + HD], axis=1, keepdims=True) for i in range(heads)]
            per = jnp.concatenate(per + [jnp.zeros((half, 128 - heads), WIDE)], axis=1)
            dd_ref[:, at : at + half] = jnp.transpose(per)[0:8]
        dqt_ref[...] = jnp.zeros_like(dqt_ref)
        lse = jnp.concatenate([lse_m_ref[...], lse_o_ref[...]], axis=1)

        def step(i, _):
            at = pl.multiple_of(i * block, block)
            bias = jnp.where(idc_ref[pl.ds(at, block), :] == idr_ref[...], 0.0, MASKED)
            dks, dvs = [], []
            for head in range(heads):
                cols = slice(head * HD, head * HD + HD)
                q = qkv_ref[:, cols]
                k = qkv_ref[pl.ds(at, block), width + head * HD : width + head * HD + HD]
                v = qkv_ref[pl.ds(at, block), 2 * width + head * HD : 2 * width + head * HD + HD]
                ga = ga_ref[:, cols]
                scaled = k * jnp.asarray(HD**-0.5, NARROW)
                p = jnp.exp(dot(scaled, q, NT) + bias - lse[head : head + 1, :])
                dvs.append(dot(p.astype(NARROW), ga))
                ds = (p * (dot(v, ga, NT) - dd_ref[head : head + 1, :])).astype(NARROW)
                dks.append(dot(ds, q) * HD**-0.5)
                dqt_ref[cols, :] += dot(scaled, ds, TN)
            d_ref[pl.ds(at, block), width : 2 * width] = jnp.concatenate(dks, axis=1).astype(NARROW)
            d_ref[pl.ds(at, block), 2 * width :] = jnp.concatenate(dvs, axis=1).astype(NARROW)
            return 0

        lax.fori_loop(0, rows // block, step, 0)
        d_ref[:, :width] = jnp.transpose(dqt_ref[...]).astype(NARROW)
        sum_ref[...] = jnp.broadcast_to(jnp.sum(d_ref[...].astype(WIDE), axis=0, keepdims=True), sum_ref.shape)
        for ref, at in ((part_o_ref, half), (part_m_ref, 0)):
            ref[...] = dot(d_ref[at : at + half, :], wq_ref[...], NT).astype(NARROW)

    return kernel


class Layout:
    def __init__(self, mesh):
        self.pairs = mesh.shape["dp"] // 2
        self.tensor = mesh.shape["tensor"]
        self.lowers = self.tensor // 2
        self.everyone = [
            (k, c, h, l)
            for k in range(self.pairs)
            for c in range(2)
            for h in range(2)
            for l in range(self.lowers)
        ]
        self.same = [a for a in self.everyone if a[1] == a[2]]
        self.cross = [a for a in self.everyone if a[1] != a[2]]

    def place(self, k, c, h, l):
        return (2 * k + c) * self.tensor + self.lowers * h + l

    def send(self, value, among, where):
        perm = [(self.place(*a), self.place(*where(*a))) for a in among]
        return lax.ppermute(value, AXES, perm)

    def to_core(self, value):
        return self.send(value, self.everyone, lambda k, c, h, l: (k, 1 - c, h, l))

    def to_lower(self, value):
        return self.send(value, self.everyone, lambda k, c, h, l: (k, c, h, 1 - l))


def here(lay):
    at = lax.axis_index("dp")
    z = lax.axis_index("tensor")
    return at // 2, at % 2, z // lay.lowers, z % lay.lowers


def in_order(pieces, number):
    pieces = list(pieces)
    bit = 1
    while bit < len(pieces):
        swap = (number & bit) != 0
        pieces = [jnp.where(swap, pieces[i ^ bit], pieces[i]) for i in range(len(pieces))]
        bit *= 2
    return pieces


def block(value, number, count):
    size = value.shape[0] // count
    return lax.dynamic_slice_in_dim(value, number * size, size, 0)


def among_pairs(lay, piece, among):
    k = here(lay)[0]
    pieces = [piece] + [
        lay.send(piece, among, lambda k, c, h, l, j=j: (k ^ j, c, h, l))
        for j in range(1, lay.pairs)
    ]
    return in_order(pieces, k)


def fetch(lay, natives):
    k, c, h, l = here(lay)
    mine = jnp.concatenate([block(w, k, lay.pairs) for w in natives], axis=1)
    got = lay.send(mine, lay.cross, lambda k, c, h, l: (k, 1 - c, 1 - h, l))
    pieces = among_pairs(lay, got, lay.cross)
    out, at = [], 0
    for w in natives:
        width = w.shape[1]
        whole = jnp.concatenate([p[:, at : at + width] for p in pieces], axis=0)
        out.append(jnp.where(c == h, w, whole))
        at += width
    return out


def total_grads(lay, grads):
    k, c, h, l = here(lay)
    cut = lambda number: jnp.concatenate([block(x, number, lay.pairs) for x in grads], axis=0)
    mine = cut(k).astype(WIDE)
    for j in range(1, lay.pairs):
        mine = mine + lay.send(
            cut(k ^ j), lay.everyone, lambda k, c, h, l, j=j: (k ^ j, c, h, l)
        ).astype(WIDE)
    mine = mine.astype(NARROW)
    got = lay.send(mine, lay.cross, lambda k, c, h, l: (k, c, 1 - h, l))
    mine = (mine.astype(WIDE) + got.astype(WIDE)).astype(NARROW)
    whole = jnp.stack(among_pairs(lay, mine, lay.same))
    other = lay.send(whole, lay.same, lambda k, c, h, l: (k, 1 - c, h, l))
    whole = jnp.where(c == h, whole, other)
    out, at = [], 0
    for x in grads:
        size = x.shape[0] // lay.pairs
        out.append(whole[:, at : at + size].reshape(x.shape))
        at += size
    return out


def total_small(lay, value):
    bits = [lambda k, c, h, l, j=1 << b: (k ^ j, c, h, l) for b in range(lay.pairs.bit_length() - 1)]
    bits += [lambda k, c, h, l: (k, c, 1 - h, l), lambda k, c, h, l: (k, 1 - c, h, l)]
    for where in bits:
        value = value + lay.send(value, lay.everyone, where)
    return value


def spread(lay, rows):
    k, c, h, l = here(lay)
    part = block(rows, l, lay.lowers)
    halves = [
        lay.send(
            part,
            [a for a in lay.everyone if a[1] == side],
            lambda k, c, h, l: (k, h, 1 - h, l),
        )
        for side in range(2)
    ]
    both = jnp.stack(halves)
    beside = lay.send(both, lay.cross, lambda k, c, h, l: (k, c, h, 1 - l))
    first = jnp.where(l == 0, both, beside)
    second = jnp.where(l == 0, beside, both)
    far = jnp.stack([first, second], axis=1).reshape(2 * rows.shape[0], rows.shape[1])
    other = lay.send(rows, lay.cross, lambda k, c, h, l: (k, 1 - c, h, l))
    near = jnp.concatenate(
        [jnp.where(c == 0, rows, other), jnp.where(c == 0, other, rows)], axis=0
    )
    return jnp.where(c == h, near, far)


def add(a, b):
    return (a.astype(WIDE) + b.astype(WIDE)).astype(NARROW)


def body(
    lay,
    tokens_in,
    patch_mask,
    image_ids,
    mask_token,
    norm1_gain,
    norm1_bias,
    qkv_weight,
    qv_bias,
    out_weight,
    out_bias,
    norm2_gain,
    norm2_bias,
    up_weight,
    up_bias,
    down_weight,
    down_bias,
    out_grad,
):
    k, c, h, l = here(lay)
    near = c == h
    layers, d, _, width = qkv_weight.shape
    hidden_units = up_weight.shape[2]
    rows_all = tokens_in.shape[0]
    half = rows_all // 2
    heads = width // HD
    block_rows = 256

    def swap_rows(native):
        mine = block(native, c, 2)
        got = lay.send(block(native, 1 - c, 2), lay.same, lambda k, c, h, l: (k, 1 - c, h, l))
        return jnp.where(near, mine, got)

    tokens = swap_rows(tokens_in)
    whole = jnp.concatenate([block(patch_mask, 1 - c, 2), image_ids])
    got = lay.send(whole, lay.same, lambda k, c, h, l: (k, 1 - c, h, l))
    masked = jnp.where(near, block(patch_mask, c, 2), got[:half])[:, None]
    ids = jnp.where(near, image_ids, got[half:])
    ids = jnp.concatenate([block(ids, c, 2), block(ids, 1 - c, 2)])
    idc, idr = ids[:, None], ids[None, :]

    natives = [
        (
            qkv_weight[i].reshape(d, 3 * width),
            up_weight[i],
            down_weight[i],
            jnp.transpose(out_weight[i]),
        )
        for i in range(layers)
    ]
    fetched = []
    for i in range(layers):
        if i == 0:
            fetched.append(fetch(lay, natives[i][:1]) + fetch(lay, natives[i][1:]))
        else:
            fetched.append(fetch(lay, natives[i]))
    biases = jnp.concatenate([up_bias, qv_bias.reshape(layers, 2 * width)], axis=1)
    got = lay.send(biases, lay.cross, lambda k, c, h, l: (k, 1 - c, 1 - h, l))
    biases = jnp.where(near, biases, got)
    b_up = [biases[i : i + 1, :hidden_units] for i in range(layers)]
    nothing = jnp.zeros((1, width), WIDE)
    b_qkv = [
        jnp.concatenate(
            [
                biases[i : i + 1, hidden_units : hidden_units + width],
                nothing,
                biases[i : i + 1, hidden_units + width :],
            ],
            axis=1,
        )
        for i in range(layers)
    ]

    rows_f = shape((half, d), WIDE)
    rows_b = shape((half, d))
    rows_u = shape((half, hidden_units))
    h_rows, n1m = call(
        first_kernel, [rows_f, rows_b], tokens, masked, mask_token[None], norm1_gain[:1], norm1_bias[:1]
    )
    kept = []
    activations = None
    for i in range(layers):
        w_qkv, w_up, w_down, w_out = fetched[i]
        n1o = lay.to_core(n1m)
        (qkv,) = call(
            qkv_kernel, [shape((rows_all, 3 * width))], n1m, n1o, w_qkv, b_qkv[i], flops=2 * rows_all * d * 3 * width
        )
        att, lse, part = [None] * 2, [None] * 2, [None] * 2
        for s in (1, 0):
            att[s], lse[s], part[s] = call(
                make_attn_fwd(s * half, s * half + half, width, block_rows),
                [shape((half, width)), shape((heads, half), WIDE), rows_b],
                qkv,
                idc,
                idr,
                w_out,
                flops=4 * half * rows_all * width * 4,
                exps=half * rows_all * heads,
            )
        mine = add(part[0], lay.to_core(part[1]))
        middle, n2m = call(
            norm_kernel,
            [rows_f, rows_b],
            h_rows,
            mine,
            lay.to_lower(mine),
            out_bias[i : i + 1],
            norm2_gain[i : i + 1],
            norm2_bias[i : i + 1],
        )
        n2 = [n2m, lay.to_core(n2m)]
        hid, slope = [None] * 2, [None] * 2
        for s in (1, 0):
            hid[s], slope[s], part[s] = call(
                mlp_kernel,
                [rows_u, rows_u, rows_b],
                n2[s],
                w_up,
                b_up[i],
                w_down,
                flops=4 * half * d * hidden_units,
                exps=2 * half * hidden_units,
            )
        mine = add(part[0], lay.to_core(part[1]))
        kept.append((h_rows, n1m, n1o, qkv, att, lse, middle, n2, hid, slope))
        j = min(i + 1, layers - 1)
        h_rows, n1m = call(
            norm_kernel,
            [rows_f, rows_b],
            middle,
            mine,
            lay.to_lower(mine),
            down_bias[i : i + 1],
            norm1_gain[j : j + 1],
            norm1_bias[j : j + 1],
        )
    activations = spread(lay, h_rows.astype(NARROW)).astype(WIDE)

    g = swap_rows(out_grad)
    rows_s = shape((half + 16, d))
    small_f = shape((8, d), WIDE)
    (glm,) = call(cast_kernel, [rows_s], g)
    big = [None] * layers
    vectors = [[None] * 8 for _ in range(layers)]

    def vector_rows(rows):
        rows = [jnp.pad(r, ((0, 0), (0, d - r.shape[1]))).astype(NARROW) for r in rows]
        return jnp.concatenate(rows + [jnp.zeros((max(16, lay.pairs) - len(rows), d), NARROW)], axis=0)

    waiting = []
    for i in reversed(range(layers)):
        h_rows, n1m, n1o, qkv, att, lse, middle, n2, hid, slope = kept[i]
        w_qkv, w_up, w_down, w_out = fetched[i]
        gl = [glm, lay.to_core(glm)]
        sums_g = gl[0][half:].astype(WIDE) + gl[1][half:].astype(WIDE)
        gb, part, sums = [None] * 2, [None] * 2, [None] * 2
        for s in (1, 0):
            gb[s], part[s], sums[s] = call(
                mlp_back_kernel,
                [rows_u, rows_b, shape((8, hidden_units), WIDE)],
                gl[s],
                w_down,
                slope[s],
                w_up,
                flops=4 * half * d * hidden_units,
            )
        mine = add(part[0], lay.to_core(part[1]))
        got = lay.to_lower(mine)
        (d_down,) = call(
            pair_grad_kernel, [shape((hidden_units, d))], hid[0], hid[1], gl[0], gl[1], flops=2 * rows_all * d * hidden_units
        )
        (d_up,) = call(
            pair_grad_kernel, [shape((d, hidden_units))], n2[0], n2[1], gb[0], gb[1], flops=2 * rows_all * d * hidden_units
        )
        mlp_rows = [sums_g[0:1], sums_g[1:2], sums_g[2:3], sums[0][:1] + sums[1][:1]]
        gm, gmm, _ = call(
            make_norm_back(False), [rows_f, rows_s, small_f], g, mine, got, middle, norm2_gain[i : i + 1]
        )
        gm2 = [gmm, lay.to_core(gmm)]
        sums_m = gm2[0][half:].astype(WIDE) + gm2[1][half:].astype(WIDE)
        dqkv, qkv_sum, part_m, part_o = call(
            make_attn_back(width, block_rows),
            [shape((rows_all, 3 * width)), shape((8, 3 * width), WIDE), rows_b, rows_b],
            gm2[0],
            gm2[1],
            w_out,
            qkv,
            att[0],
            att[1],
            lse[0],
            lse[1],
            idc,
            idr,
            w_qkv,
            scratch=[
                pltpu.VMEM((rows_all, width), NARROW),
                pltpu.VMEM((width, rows_all), WIDE),
                pltpu.VMEM((8, rows_all), WIDE),
            ],
            flops=10 * rows_all * rows_all * width * 4,
            exps=rows_all * rows_all * heads,
        )
        mine = add(part_m, lay.to_core(part_o))
        got = lay.to_lower(mine)
        (d_out,) = call(
            pair_grad_kernel, [shape((width, d))], att[0], att[1], gm2[0], gm2[1], flops=2 * rows_all * d * width
        )
        (d_qkv,) = call(
            pair_grad_kernel,
            [shape((3 * width, d))],
            dqkv[:half],
            dqkv[half:],
            n1m,
            n1o,
            flops=2 * rows_all * d * 3 * width,
        )
        att_rows = [
            sums_m[0:1],
            sums_m[1:2],
            sums_m[2:3],
            jnp.concatenate([qkv_sum[:1, :width], qkv_sum[:1, 2 * width :]], axis=1),
        ]
        if i:
            big[i] = total_grads(lay, [d_down, d_up, d_out, d_qkv, vector_rows(mlp_rows + att_rows)])
            vectors[i] = big[i].pop()
            g, glm, _ = call(
                make_norm_back(False), [rows_f, rows_s, small_f], gm, mine, got, h_rows, norm1_gain[i : i + 1]
            )
        else:
            one = total_grads(lay, [d_down, d_up, vector_rows(mlp_rows)])
            two = total_grads(lay, [d_out, d_qkv, vector_rows(att_rows)])
            vectors[i] = jnp.concatenate([one.pop()[:4], two.pop()[:4]], axis=0)
            big[i] = one + two
            tok, last = call(
                make_norm_back(True), [rows_b, small_f], gm, mine, got, h_rows, norm1_gain[:1], masked
            )
    tokens_grad = spread(lay, tok).astype(WIDE)
    last = total_small(lay, last)

    vec = [v.astype(WIDE) for v in vectors]
    after = [last[0:2]] + [vec[i][0:2] for i in range(layers)]
    d_gain1 = jnp.stack([after[0][0]] + [vec[i][0] for i in range(layers - 1)])
    d_shift1 = jnp.stack([after[0][1]] + [vec[i][1] for i in range(layers - 1)])
    every = jnp.stack([v[:8] for v in vec])
    full = [jnp.stack([big[i][n] for i in range(layers)]).astype(WIDE) for n in range(4)]
    d_qkv = jnp.stack([jnp.transpose(big[i][3]).astype(WIDE) for i in range(layers)])
    return (
        activations,
        tokens_grad,
        last[2],
        d_gain1,
        d_shift1,
        d_qkv.reshape(layers, d, 3, width),
        every[:, 7, : 2 * width].reshape(layers, 2, width),
        full[2],
        every[:, 6],
        every[:, 4],
        every[:, 5],
        full[1],
        every[:, 3, :hidden_units],
        full[0],
        every[:, 2],
    )


def solution(mesh):
    lay = Layout(mesh)
    placed = (
        P("dp", None),
        P("dp"),
        P("dp"),
        P(),
        P(),
        P(),
        P(None, None, None, "tensor"),
        P(None, None, "tensor"),
        P(None, "tensor", None),
        P(),
        P(),
        P(),
        P(None, None, "tensor"),
        P(None, "tensor"),
        P(None, "tensor", None),
        P(),
        P("dp", None),
    )
    return jax.shard_map(
        partial(body, lay),
        mesh=mesh,
        in_specs=placed,
        out_specs=(
            P("dp", None),
            P("dp", None),
            P(),
            P(),
            P(),
            P(None, None, None, "tensor"),
            P(None, None, "tensor"),
            P(None, "tensor", None),
            P(),
            P(),
            P(),
            P(None, None, "tensor"),
            P(None, "tensor"),
            P(None, "tensor", None),
            P(),
        ),
        check_vma=False,
    )
```

time: 894 us -> 551 us (0.62)
  waiting for transfers between devices: 556 us -> 143 us
  starting transfers between devices: 1.53 us -> 149 us
  matrix products: 126 us -> 0 us
  Pallas kernels: 0 us -> 99.9 us
  other arithmetic: 109 us -> 55.8 us
  local copies, waits for them, and re-layouts: 52.5 us -> 92.1 us
  blocking collectives: 22.8 us -> 0 us
  between operations: 16.2 us -> 3.82 us
    psum x8 -> x0, waiting for transfers between devices: 556 us -> none  [the longest x4 292 us: branch_total(): lax.psum(partial_sum.astype(jnp.bfloat16), 'tensor').astype(jnp.float32)]
    ppermute x0 -> x76, starting transfers between devices: none -> 149 us  [send(): return lax.ppermute(value, AXES, perm)]
    ppermute x0 -> x76, waiting for transfers between devices: none -> 143 us  [send(): return lax.ppermute(value, AXES, perm)]
    dot_general x48 -> x0, matrix products: 121 us -> none  [the longest x2 29.3 us: body(): jnp.dot(normed_mid, up_weight[layer_at], preferred_element_type=WIDE)]
    pallas_call x0 -> x34, Pallas kernels: none -> 99.9 us  [call(): pl.pallas_call(kernel, out_shape=outs, in_specs=[pl.BlockSpec(memory_spac...]
    reduce_sum x30 -> x0, other arithmetic: 59.4 us -> none  [the longest x12 23.8 us: layer_norm(): return centre * lax.rsqrt(spread + EPSILON) * gain_row + shift_row]
    slice x11 -> x57, local copies, waits for them, and re-layouts: 5.98 us -> 30.3 us  [the longest x20 13.5 us: fetch(): whole = jnp.concatenate([p[:, at:at + width] for p in pieces], axis=0)]
    psum x1 -> x0, blocking collectives: 22.8 us -> none  [body(): lax.psum(fill_grad.astype(jnp.bfloat16), 'dp').astype(jnp.float32)]
  transfers between devices with their start and end apart: 8 -> 76, of which waited for: 8 -> 21; matrix products, arithmetic and copies ran while one was open for 7% -> 17% of each run, Pallas kernels for 0% -> 16%
where the time goes in v1:
time: 551 us; the launch traced here: 544 us
  starting transfers between devices  149 us (27%)
  waiting for transfers between devices  143 us (26%)
  Pallas kernels  99.9 us (18%)
  local copies, waits for them, and re-layouts  92.1 us (17%)
  other arithmetic  55.8 us (10%)
    ppermute x76, starting transfers between devices, send(): return lax.ppermute(value, AXES, perm)  149 us
    ppermute x76, waiting for transfers between devices, send(): return lax.ppermute(value, AXES, perm)  143 us
    pallas_call x34, Pallas kernels, call(): pl.pallas_call(kernel, out_shape=outs, in_specs=[pl.BlockSpec(memory_spac...  99.9 us
    unnamed x308, local copies, waits for them, and re-layouts  38 us
    slice x20, local copies, waits for them, and re-layouts, fetch(): whole = jnp.concatenate([p[:, at:at + width] for p in pieces], axis=0)  13.5 us
  transfers between devices with their start and end apart: 76, of which 21 were waited for; matrix products, arithmetic and copies ran while one was open for 17% of the time, Pallas kernels for 16%

profile of v1, /device:TPU:1, one launch (start us, length us, event | category | flops | bytes accessed | tf_op | source)
XLA Modules:
  0.0 543.7 jit_solution(15807942777720670558)
XLA Ops:
  4.9 5.6 %collective-permute-start.7 = (f32[2,1152]{1,0:T(2,128)S(1)}, f32[2,1152]{1,0:T(2,128)S(1)}, u32[]{:S(2)}, u32[]{:S(2)}) collective-permute-start(f32[2,1152]{1,0:T(2,128)S(1)} %constant_dynamic-update-slice_fusion), channel_id=1, source_target_pairs={{2,4},{3,5},{4,2},{5,3},{10,12},{11,13},{12,10},{13,11},{18,20},{1... | collective-permute-start | bytes 27656 | tf_op jit(solution)/shard_map/ppermute | solution.py:281
  25.0 4.7 collective-permute-start.8
  60.0 8.8 %collective-permute-done.18 = bf16[192,2304]{1,0:T(8,128)(2,1)S(1)} collective-permute-done((bf16[192,2304]{1,0:T(8,128)(2,1)}, bf16[192,2304]{1,0:T(8,128)(2,1)S(1)}, u32[]{:S(2)}, u32[]{:S(2)}) %collective-permute-start.18) | collective-permute-done | bytes 884768 | tf_op jit(solution)/shard_map/ppermute | solution.py:281
  83.2 5.2 shard_map.283
  88.5 5.2 shard_map.282
  102.2 15.7 %collective-permute-done.13.b_ref = bf16[512,768]{1,0:T(8,128)(2,1)S(1)} collective-permute-done((bf16[512,768]{1,0:T(8,128)(2,1)S(1)}, bf16[512,768]{1,0:T(8,128)(2,1)S(1)}, u32[]{:S(2)}, u32[]{:S(2)}) %collective-permute-start.13) | collective-permute-done | bytes 786464 | tf_op jit(solution)/shard_map/ppermute | solution.py:281
  131.9 19.1 %collective-permute-done.16.b_ref = bf16[512,768]{1,0:T(8,128)(2,1)S(1)} collective-permute-done((bf16[512,768]{1,0:T(8,128)(2,1)S(1)}, bf16[512,768]{1,0:T(8,128)(2,1)S(1)}, u32[]{:S(2)}, u32[]{:S(2)}) %collective-permute-start.16) | collective-permute-done | bytes 786464 | tf_op jit(solution)/shard_map/ppermute | solution.py:281
  164.3 5.2 shard_map.290
  172.7 5.6 %shard_map.289 = (bf16[512,192]{1,0:T(8,128)(2,1)S(1)}, f32[3,512]{1,0:T(4,128)S(1)}, bf16[512,768]{1,0:T(8,128)(2,1)S(1)}) custom-call(bf16[1024,576]{1,0:T(8,128)(2,1)S(1)} %shard_map.288.qkv_ref, s32[1024,1]{1,0:T(8,128)S(1)} %copy.56.idc_ref, s32[1,1024]{1,0:T(1,128)S(1)} %bitcast.116, bf16[768,192]{1,0:T(8,128)(2,1)S(1)} %maximum_select_fusion.9.w_ref), custom_call_target="tpu_custom_call" | custom-call | flops 1610612736 | bytes 2471936 | tf_op jit(solution)/shard_map/pallas_call | solution.py:28
  178.6 17.8 %collective-permute-done.23.b_ref = bf16[512,768]{1,0:T(8,128)(2,1)S(1)} collective-permute-done((bf16[512,768]{1,0:T(8,128)(2,1)S(1)}, bf16[512,768]{1,0:T(8,128)(2,1)S(1)}, u32[]{:S(2)}, u32[]{:S(2)}) %collective-permute-start.23) | collective-permute-done | bytes 786464 | tf_op jit(solution)/shard_map/ppermute | solution.py:281
  222.6 11.3 %collective-permute-done.34.b_ref = bf16[512,768]{1,0:T(8,128)(2,1)} collective-permute-done((bf16[512,768]{1,0:T(8,128)(2,1)}, bf16[512,768]{1,0:T(8,128)(2,1)}, u32[]{:S(2)}, u32[]{:S(2)}) %collective-permute-start.34) | collective-permute-done | bytes 786464 | tf_op jit(solution)/shard_map/ppermute | solution.py:281
  244.5 14.0 %shard_map.299 = (bf16[1024,576]{1,0:T(8,128)(2,1)}, f32[8,576]{1,0:T(8,128)S(1)}, bf16[512,768]{1,0:T(8,128)(2,1)S(1)}, bf16[512,768]{1,0:T(8,128)(2,1)S(1)}) custom-call(bf16[528,768]{1,0:T(8,128)(2,1)S(1)} %get-tuple-element.98.gm_ref.bm_ref, bf16[528,768]{1,0:T(8,128)(2,1)S(1)} %collective-permute-done.35.go_ref.bo_ref, bf16[768,192]{1,0:T(8,128)(2,1)S(1)} %copy-done.43, ...), custom_call_target="tpu_custom_call" | custom-call | flops 8053063680 | bytes 7165952 | tf_op jit(solution)/shard_map/pallas_call | solution.py:28
  270.1 13.3 %collective-permute-done.37.b_ref = bf16[512,768]{1,0:T(8,128)(2,1)S(1)} collective-permute-done((bf16[512,768]{1,0:T(8,128)(2,1)S(1)}, bf16[512,768]{1,0:T(8,128)(2,1)S(1)}, u32[]{:S(2)}, u32[]{:S(2)}) %collective-permute-start.37) | collective-permute-done | bytes 786464 | tf_op jit(solution)/shard_map/ppermute | solution.py:281
  305.1 4.6 collective-permute-done.69
  323.9 7.8 %collective-permute-done.28 = bf16[256,768]{1,0:T(8,128)(2,1)} collective-permute-done((bf16[256,768]{1,0:T(8,128)(2,1)}, bf16[256,768]{1,0:T(8,128)(2,1)}, u32[]{:S(2)}, u32[]{:S(2)}) %collective-permute-start.28) | collective-permute-done | bytes 393248 | tf_op jit(solution)/shard_map/ppermute | solution.py:281
  363.4 7.0 %collective-permute-start.41 = (bf16[528,768]{1,0:T(8,128)(2,1)S(1)}, bf16[528,768]{1,0:T(8,128)(2,1)S(1)}, u32[]{:S(2)}, u32[]{:S(2)}) collective-permute-start(bf16[528,768]{1,0:T(8,128)(2,1)S(1)} %get-tuple-element.112.gm_ref.bm_ref), channel_id=1, source_target_pairs={{0,4},{1,5},{2,6},{3,7},{4,0},{5,1},{6,2},{7,3},{8,12},{9,13},{10,... | collective-permute-start | bytes 2433032 | tf_op jit(solution)/shard_map/ppermute | solution.py:281
  379.2 13.7 %shard_map.304 = (bf16[1024,576]{1,0:T(8,128)(2,1)}, f32[8,576]{1,0:T(8,128)S(1)}, bf16[512,768]{1,0:T(8,128)(2,1)S(1)}, bf16[512,768]{1,0:T(8,128)(2,1)S(1)}) custom-call(bf16[528,768]{1,0:T(8,128)(2,1)S(1)} %get-tuple-element.112.gm_ref.bm_ref, bf16[528,768]{1,0:T(8,128)(2,1)S(1)} %collective-permute-done.41.go_ref.bo_ref, ...), custom_call_target="tpu_custom_call" | custom-call | flops 8053063680 | bytes 7165952 | tf_op jit(solution)/shard_map/pallas_call | solution.py:28
  409.6 9.1 %collective-permute-start.63 = (bf16[196,768]{1,0:T(8,128)(2,1)S(1)}, bf16[196,768]{1,0:T(8,128)(2,1)S(1)}, u32[]{:S(2)}, u32[]{:S(2)}) collective-permute-start(bf16[196,768]{1,0:T(8,128)(2,1)S(1)} %add_convert_fusion.13), channel_id=1, source_target_pairs={{2,0},{3,1},{4,6},{5,7},{10,8},{11,9},{12,14},{13,15},{18,16},{19,... | collective-permute-start | bytes 903176 | tf_op jit(solution)/shard_map/ppermute | solution.py:281
  425.0 7.7 %collective-permute-done.52 = bf16[388,768]{1,0:T(8,128)(2,1)S(1)} collective-permute-done((bf16[388,768]{1,0:T(8,128)(2,1)S(1)}, bf16[388,768]{1,0:T(8,128)(2,1)S(1)}, u32[]{:S(2)}, u32[]{:S(2)}) %collective-permute-start.52) | collective-permute-done | bytes 596000 | tf_op jit(solution)/shard_map/ppermute | solution.py:281
  434.2 9.3 %collective-permute-done.53 = bf16[388,768]{1,0:T(8,128)(2,1)S(1)} collective-permute-done((bf16[388,768]{1,0:T(8,128)(2,1)S(1)}, bf16[388,768]{1,0:T(8,128)(2,1)S(1)}, u32[]{:S(2)}, u32[]{:S(2)}) %collective-permute-start.53) | collective-permute-done | bytes 596000 | tf_op jit(solution)/shard_map/ppermute | solution.py:281
  465.2 21.8 %collective-permute-start.50 = (f32[8,768]{1,0:T(8,128)S(1)}, f32[8,768]{1,0:T(8,128)S(1)}, u32[]{:S(2)}, u32[]{:S(2)}) collective-permute-start(f32[8,768]{1,0:T(8,128)S(1)} %add.227), channel_id=1, source_target_pairs={{0,2},{1,3},{2,0},{3,1},{4,6},{5,7},{6,4},{7,5},{8,10},{9,11},{10,... | collective-permute-start | bytes 73736 | tf_op jit(solution)/shard_map/ppermute | solution.py:281
  488.3 4.7 collective-permute-start.46
  502.3 4.7 collective-permute-start.44
  519.0 5.4 collective-permute-done.47
  (649 shorter events, 312.4 us)
Async XLA Ops:
  2.1 32.6 %collective-permute-start.1 = (s32[1536]{0:T(1024)S(1)}, s32[1536]{0:T(1024)S(1)}, u32[]{:S(2)}, u32[]{:S(2)}) collective-permute-start(s32[1536]{0:T(1024)S(1)} %pad_add_fusion), channel_id=1, source_target_pairs={{0,4},{1,5},{6,2},{7,3},{8,12},{9,13},{14,10},{15,11},{16,20},{17,... | collective-permute-start | bytes 18440 | tf_op jit(solution)/shard_map/ppermute | solution.py:281
  4.9 30.4 %collective-permute-start.7 = (f32[2,1152]{1,0:T(2,128)S(1)}, f32[2,1152]{1,0:T(2,128)S(1)}, u32[]{:S(2)}, u32[]{:S(2)}) collective-permute-start(f32[2,1152]{1,0:T(2,128)S(1)} %constant_dynamic-update-slice_fusion), channel_id=1, source_target_pairs={{2,4},{3,5},{4,2},{5,3},{10,12},{11,13},{12,10},{13,11},{18,20},{1... | collective-permute-start | bytes 27656 | tf_op jit(solution)/shard_map/ppermute | solution.py:281
  12.6 43.8 %collective-permute-start = (bf16[512,768]{1,0:T(8,128)(2,1)}, bf16[512,768]{1,0:T(8,128)(2,1)}, u32[]{:S(2)}, u32[]{:S(2)}) collective-permute-start(bf16[512,768]{1,0:T(8,128)(2,1)} %constant_dynamic-slice_fusion.33), channel_id=1, source_target_pairs={{0,4},{1,5},{6,2},{7,3},{8,12},{9,13},{14,10},{15,11},{16,20},{17,... | collective-permute-start | bytes 2359304 | tf_op jit(solution)/shard_map/ppermute | solution.py:281
  46.6 25.3 %collective-permute-start.11 = (bf16[192,1728]{1,0:T(8,128)(2,1)}, bf16[192,1728]{1,0:T(8,128)(2,1)S(1)}, u32[]{:S(2)}, u32[]{:S(2)}) collective-permute-start(bf16[192,1728]{1,0:T(8,128)(2,1)} %collective-permute-done.8), channel_id=1, source_target_pairs={{2,10},{3,11},{4,12},{5,13},{10,2},{11,3},{12,4},{13,5},{18,26},{1... | collective-permute-start | bytes 1990664 | tf_op jit(solution)/shard_map/ppermute | solution.py:281
  49.7 25.3 %collective-permute-start.10 = (bf16[192,1728]{1,0:T(8,128)(2,1)}, bf16[192,1728]{1,0:T(8,128)(2,1)S(1)}, u32[]{:S(2)}, u32[]{:S(2)}) collective-permute-start(bf16[192,1728]{1,0:T(8,128)(2,1)} %collective-permute-done.8), channel_id=1, source_target_pairs={{2,18},{3,19},{4,20},{5,21},{10,26},{11,27},{12,28},{13,29},{18,2}... | collective-permute-start | bytes 1990664 | tf_op jit(solution)/shard_map/ppermute | solution.py:281
  171.3 28.1 %collective-permute-start.31 = (f32[512,768]{1,0:T(8,128)}, f32[512,768]{1,0:T(8,128)S(1)}, u32[]{:S(2)}, u32[]{:S(2)}) collective-permute-start(f32[512,768]{1,0:T(8,128)} %constant_dynamic-slice_fusion.29), channel_id=1, source_target_pairs={{0,4},{1,5},{6,2},{7,3},{8,12},{9,13},{14,10},{15,11},{16,20},{17,... | collective-permute-start | bytes 4718600 | tf_op jit(solution)/shard_map/ppermute | solution.py:281
  215.7 26.6 %collective-permute-start.25 = (bf16[512,768]{1,0:T(8,128)(2,1)}, bf16[512,768]{1,0:T(8,128)(2,1)S(1)}, u32[]{:S(2)}, u32[]{:S(2)}) collective-permute-start(bf16[512,768]{1,0:T(8,128)(2,1)} %copy-done.60), channel_id=1, source_target_pairs={{0,4},{1,5},{2,6},{3,7},{4,0},{5,1},{6,2},{7,3},{8,12},{9,13},{10,... | collective-permute-start | bytes 2359304 | tf_op jit(solution)/shard_map/ppermute | solution.py:281
  244.5 49.3 %collective-permute-start.26 = (bf16[512,768]{1,0:T(8,128)(2,1)}, bf16[512,768]{1,0:T(8,128)(2,1)}, u32[]{:S(2)}, u32[]{:S(2)}) collective-permute-start(bf16[512,768]{1,0:T(8,128)(2,1)} %add_convert_fusion.6.a_ref), channel_id=1, source_target_pairs={{0,1},{1,0},{2,3},{3,2},{4,5},{5,4},{6,7},{7,6},{8,9},{9,8},{10,11... | collective-permute-start | bytes 2359304 | tf_op jit(solution)/shard_map/ppermute | solution.py:281
  267.5 36.3 %collective-permute-start.70 = (bf16[580,768]{1,0:T(8,128)(2,1)}, bf16[580,768]{1,0:T(8,128)(2,1)}, u32[]{:S(2)}, u32[]{:S(2)}) collective-permute-start(bf16[580,768]{1,0:T(8,128)(2,1)} %get-tuple-element.247), channel_id=1, source_target_pairs={{0,24},{1,25},{2,26},{3,27},{4,28},{5,29},{6,30},{7,31},{8,16},{9,... | collective-permute-start | bytes 2672648 | tf_op jit(solution)/shard_map/ppermute | solution.py:281
  268.7 41.1 %collective-permute-start.69 = (bf16[580,768]{1,0:T(8,128)(2,1)}, bf16[580,768]{1,0:T(8,128)(2,1)}, u32[]{:S(2)}, u32[]{:S(2)}) collective-permute-start(bf16[580,768]{1,0:T(8,128)(2,1)} %get-tuple-element.248), channel_id=1, source_target_pairs={{0,16},{1,17},{2,18},{3,19},{4,20},{5,21},{6,22},{7,23},{8,24},{9,... | collective-permute-start | bytes 2672648 | tf_op jit(solution)/shard_map/ppermute | solution.py:281
  268.9 44.1 %collective-permute-start.68 = (bf16[580,768]{1,0:T(8,128)(2,1)}, bf16[580,768]{1,0:T(8,128)(2,1)}, u32[]{:S(2)}, u32[]{:S(2)}) collective-permute-start(bf16[580,768]{1,0:T(8,128)(2,1)} %get-tuple-element.249), channel_id=1, source_target_pairs={{0,8},{1,9},{2,10},{3,11},{4,12},{5,13},{6,14},{7,15},{8,0},{9,1},... | collective-permute-start | bytes 2672648 | tf_op jit(solution)/shard_map/ppermute | solution.py:281
  292.9 25.8 %collective-permute-start.38 = (bf16[528,768]{1,0:T(8,128)(2,1)}, bf16[528,768]{1,0:T(8,128)(2,1)}, u32[]{:S(2)}, u32[]{:S(2)}) collective-permute-start(bf16[528,768]{1,0:T(8,128)(2,1)} %get-tuple-element.106.g_ref.bm_ref), channel_id=1, source_target_pairs={{0,4},{1,5},{2,6},{3,7},{4,0},{5,1},{6,2},{7,3},{8,12},{9,13},{10,... | collective-permute-start | bytes 2433032 | tf_op jit(solution)/shard_map/ppermute | solution.py:281
  303.8 27.9 %collective-permute-start.28 = (bf16[256,768]{1,0:T(8,128)(2,1)}, bf16[256,768]{1,0:T(8,128)(2,1)}, u32[]{:S(2)}, u32[]{:S(2)}) collective-permute-start(bf16[256,768]{1,0:T(8,128)(2,1)} %constant_dynamic-slice_fusion.30), channel_id=1, source_target_pairs={{0,2},{1,3},{2,4},{3,5},{8,10},{9,11},{10,12},{11,13},{16,18},{17,... | collective-permute-start | bytes 1179656 | tf_op jit(solution)/shard_map/ppermute | solution.py:281
  309.7 26.1 %collective-permute-start.27 = (bf16[512,768]{1,0:T(8,128)(2,1)}, bf16[512,768]{1,0:T(8,128)(2,1)}, u32[]{:S(2)}, u32[]{:S(2)}) collective-permute-start(bf16[512,768]{1,0:T(8,128)(2,1)} %convert_element_type.247), channel_id=1, source_target_pairs={{2,6},{3,7},{4,0},{5,1},{10,14},{11,15},{12,8},{13,9},{18,22},{19,... | collective-permute-start | bytes 2359304 | tf_op jit(solution)/shard_map/ppermute | solution.py:281
  342.6 28.8 %collective-permute-start.74 = (bf16[580,768]{1,0:T(8,128)(2,1)S(1)}, bf16[580,768]{1,0:T(8,128)(2,1)S(1)}, u32[]{:S(2)}, u32[]{:S(2)}) collective-permute-start(bf16[580,768]{1,0:T(8,128)(2,1)S(1)} %add_convert_fusion), channel_id=1, source_target_pairs={{0,8},{1,9},{6,14},{7,15},{8,0},{9,1},{14,6},{15,7},{16,24},{17,25... | collective-permute-start | bytes 2672648 | tf_op jit(solution)/shard_map/ppermute | solution.py:281
  343.3 28.0 %collective-permute-start.73 = (bf16[580,768]{1,0:T(8,128)(2,1)S(1)}, bf16[580,768]{1,0:T(8,128)(2,1)S(1)}, u32[]{:S(2)}, u32[]{:S(2)}) collective-permute-start(bf16[580,768]{1,0:T(8,128)(2,1)S(1)} %add_convert_fusion), channel_id=1, source_target_pairs={{0,16},{1,17},{6,22},{7,23},{8,24},{9,25},{14,30},{15,31},{16,0},{... | collective-permute-start | bytes 2672648 | tf_op jit(solution)/shard_map/ppermute | solution.py:281
  344.1 27.3 %collective-permute-start.72 = (bf16[580,768]{1,0:T(8,128)(2,1)S(1)}, bf16[580,768]{1,0:T(8,128)(2,1)S(1)}, u32[]{:S(2)}, u32[]{:S(2)}) collective-permute-start(bf16[580,768]{1,0:T(8,128)(2,1)S(1)} %add_convert_fusion), channel_id=1, source_target_pairs={{0,24},{1,25},{6,30},{7,31},{8,16},{9,17},{14,22},{15,23},{16,8},{... | collective-permute-start | bytes 2672648 | tf_op jit(solution)/shard_map/ppermute | solution.py:281
  376.8 85.1 %collective-permute-start.75 = (bf16[4,580,768]{2,0,1:T(4,128)(2,1)}, bf16[4,580,768]{2,0,1:T(4,128)(2,1)}, u32[]{:S(2)}, u32[]{:S(2)}) collective-permute-start(bf16[4,580,768]{2,0,1:T(4,128)(2,1)} %copy.72), channel_id=1, source_target_pairs={{0,4},{1,5},{6,2},{7,3},{8,12},{9,13},{14,10},{15,11},{16,20},{17,... | collective-permute-start | bytes 10690568 | tf_op jit(solution)/shard_map/ppermute | solution.py:281
  424.1 26.3 %collective-permute-start.66 = (bf16[196,768]{1,0:T(8,128)(2,1)S(1)}, bf16[196,768]{1,0:T(8,128)(2,1)S(1)}, u32[]{:S(2)}, u32[]{:S(2)}) collective-permute-start(bf16[196,768]{1,0:T(8,128)(2,1)S(1)} %add_convert_fusion.12), channel_id=1, source_target_pairs={{0,8},{1,9},{6,14},{7,15},{8,0},{9,1},{14,6},{15,7},{16,24},{17,25... | collective-permute-start | bytes 903176 | tf_op jit(solution)/shard_map/ppermute | solution.py:281
  455.1 58.5 %collective-permute-start.67 = (bf16[4,196,768]{2,0,1:T(4,128)(2,1)}, bf16[4,196,768]{2,0,1:T(4,128)(2,1)}, u32[]{:S(2)}, u32[]{:S(2)}) collective-permute-start(bf16[4,196,768]{2,0,1:T(4,128)(2,1)} %copy.70), channel_id=1, source_target_pairs={{0,4},{1,5},{6,2},{7,3},{8,12},{9,13},{14,10},{15,11},{16,20},{17,... | collective-permute-start | bytes 3612680 | tf_op jit(solution)/shard_map/ppermute | solution.py:281
  458.4 34.6 %collective-permute-start.58 = (bf16[388,768]{1,0:T(8,128)(2,1)S(1)}, bf16[388,768]{1,0:T(8,128)(2,1)S(1)}, u32[]{:S(2)}, u32[]{:S(2)}) collective-permute-start(bf16[388,768]{1,0:T(8,128)(2,1)S(1)} %add_convert_fusion.10), channel_id=1, source_target_pairs={{0,8},{1,9},{6,14},{7,15},{8,0},{9,1},{14,6},{15,7},{16,24},{17,25... | collective-permute-start | bytes 1787912 | tf_op jit(solution)/shard_map/ppermute | solution.py:281
  459.2 35.1 %collective-permute-start.57 = (bf16[388,768]{1,0:T(8,128)(2,1)S(1)}, bf16[388,768]{1,0:T(8,128)(2,1)S(1)}, u32[]{:S(2)}, u32[]{:S(2)}) collective-permute-start(bf16[388,768]{1,0:T(8,128)(2,1)S(1)} %add_convert_fusion.10), channel_id=1, source_target_pairs={{0,16},{1,17},{6,22},{7,23},{8,24},{9,25},{14,30},{15,31},{16,0},{... | collective-permute-start | bytes 1787912 | tf_op jit(solution)/shard_map/ppermute | solution.py:281
  461.2 34.3 %collective-permute-start.56 = (bf16[388,768]{1,0:T(8,128)(2,1)S(1)}, bf16[388,768]{1,0:T(8,128)(2,1)S(1)}, u32[]{:S(2)}, u32[]{:S(2)}) collective-permute-start(bf16[388,768]{1,0:T(8,128)(2,1)S(1)} %add_convert_fusion.10), channel_id=1, source_target_pairs={{0,24},{1,25},{6,30},{7,31},{8,16},{9,17},{14,22},{15,23},{16,8},{... | collective-permute-start | bytes 1787912 | tf_op jit(solution)/shard_map/ppermute | solution.py:281
  499.4 28.8 %collective-permute-start.59 = (bf16[4,388,768]{2,0,1:T(4,128)(2,1)}, bf16[4,388,768]{2,0,1:T(4,128)(2,1)}, u32[]{:S(2)}, u32[]{:S(2)}) collective-permute-start(bf16[4,388,768]{2,0,1:T(4,128)(2,1)} %copy.68), channel_id=1, source_target_pairs={{0,4},{1,5},{6,2},{7,3},{8,12},{9,13},{14,10},{15,11},{16,20},{17,... | collective-permute-start | bytes 7151624 | tf_op jit(solution)/shard_map/ppermute | solution.py:281
  (204 other events, 1692.1 us)
